TPU v7x, 256 devices: a whole 4x4x8 slice. The times are simulated.
256 devices in a mesh: band: 8 (over x, z_hi), grid: 32 (over z_lo, y, core).
Axes of the slice: x: 4, y: 4, z: 8 (z_hi: 2, z_lo: 4; z = z_hi * 4 + z_lo), core: 2. Of those that a mesh axis runs over, the one named last changes fastest.
Arguments:
- occupied: bfloat16 [128, 64, 64, 64], P(None, 'grid'), may hold values from -6 to 6
- empty: bfloat16 [128, 64, 64, 64], P(None, 'grid'), may hold values from -6 to 6
- pair_occ: int32 [512], P('band'), may hold values from 0 to 127
- pair_emp: int32 [512], P('band'), may hold values from 0 to 127
- g_cell: int32 [122880], P('grid'), may hold values from 0 to 8191, as said below
- eigvecs: bfloat16 [2, 122880, 2048], P(None, 'grid', 'band'), may hold values from -0.015625 to 0.015625
Outputs:
- projections: float32 [2, 512, 2048], P(None, 'grid', 'band')
Inputs may be any that keep to these rules, and one draw needn't show every extreme that they name: `g_cell`: within each aligned block of 3840 entries the values are distinct, and 0 and 8191 are among them.
All inputs are finite; a program needn't handle non-finite values.
Results may differ from a plain program's by a relative error of at most 0.0029.
Values may be sent and summed in bfloat16 or wider, within the bound.
A program may use at most 128 MiB of HBM per device.

v0:
```python
import math

import jax
import jax.numpy as jnp
from jax import lax
from jax.sharding import PartitionSpec as P

NX = 64
NY = 64
NZ = 64


TRANSFORM_PRECISION = lax.Precision.HIGH


def tables(length):
    indices = jnp.arange(length, dtype=jnp.int32)
    angles = (indices[:, None] * indices[None, :] % length).astype(jnp.float32) * (
        2.0 * math.pi / length
    )
    return (jnp.cos(angles), jnp.sin(angles))


def planes(density):
    count, slab, rows_y, rows_z = density.shape
    cos_z, sin_z = tables(rows_z)
    real_z = jnp.einsum("pxyz,zk->pxyk", density, cos_z, precision=TRANSFORM_PRECISION)
    imag_z = -jnp.einsum("pxyz,zk->pxyk", density, sin_z, precision=TRANSFORM_PRECISION)
    cos_y, sin_y = tables(rows_y)
    real_y = jnp.einsum("pxyk,yj->pxjk", real_z, cos_y, precision=TRANSFORM_PRECISION) + jnp.einsum(
        "pxyk,yj->pxjk", imag_z, sin_y, precision=TRANSFORM_PRECISION
    )
    imag_y = jnp.einsum("pxyk,yj->pxjk", imag_z, cos_y, precision=TRANSFORM_PRECISION) - jnp.einsum(
        "pxyk,yj->pxjk", real_z, sin_y, precision=TRANSFORM_PRECISION
    )
    return jnp.stack([real_y, imag_y]).reshape(2, count, slab, rows_y * rows_z)


def columns(strips, cell_map, factor):
    count = strips.shape[1]
    length = strips.shape[2]
    width = strips.shape[3]
    cos_x, sin_x = tables(length)
    real_x = jnp.einsum(
        "pxq,xk->pkq", strips[0], cos_x, precision=TRANSFORM_PRECISION
    ) + jnp.einsum("pxq,xk->pkq", strips[1], sin_x, precision=TRANSFORM_PRECISION)
    imag_x = jnp.einsum(
        "pxq,xk->pkq", strips[1], cos_x, precision=TRANSFORM_PRECISION
    ) - jnp.einsum("pxq,xk->pkq", strips[0], sin_x, precision=TRANSFORM_PRECISION)
    real_sel = jnp.take(real_x.reshape(count, length * width), cell_map, axis=1) * factor
    imag_sel = jnp.take(imag_x.reshape(count, length * width), cell_map, axis=1) * factor
    return jnp.stack([real_sel, imag_sel]).astype(jnp.bfloat16)


def project(spectra, vectors):
    real_out = jnp.dot(spectra[0], vectors[0], preferred_element_type=jnp.float32) + jnp.dot(
        spectra[1], vectors[1], preferred_element_type=jnp.float32
    )
    imag_out = jnp.dot(spectra[0], vectors[1], preferred_element_type=jnp.float32) - jnp.dot(
        spectra[1], vectors[0], preferred_element_type=jnp.float32
    )
    return jnp.stack([real_out, imag_out])


def shards(occupied, empty, pair_occ, pair_emp, g_cell, eigvecs):
    density = jnp.take(occupied, pair_occ, axis=0).astype(jnp.float32) * jnp.take(
        empty, pair_emp, axis=0
    ).astype(jnp.float32)
    factor = 1.0 / math.sqrt(NX * NY * NZ)
    spectra = columns(
        lax.all_to_all(planes(density), "grid", split_axis=3, concat_axis=2, tiled=True),
        g_cell,
        factor,
    )
    partial_sums = project(lax.all_gather(spectra, "band", axis=1, tiled=True), eigvecs)
    return lax.psum_scatter(partial_sums, "grid", scatter_dimension=1, tiled=True)


def solution(mesh):
    in_specs = (
        P(None, "grid", None, None),
        P(None, "grid", None, None),
        P("band"),
        P("band"),
        P("grid"),
        P(None, "grid", "band"),
    )
    out_specs = P(None, "grid", "band")
    return jax.shard_map(shards, mesh=mesh, in_specs=in_specs, out_specs=out_specs, check_vma=False)
```

profile of v0, /device:TPU:2, one launch (start us, length us, event | category | flops | bytes accessed | tf_op | source)
XLA Modules:
  0.0 597.5 jit_solution(3123560917683129581)
XLA Ops:
  8.7 7.5 %copy.56 = bf16[128,2,64,64]{3,2,1,0:T(8,128)(2,1)} copy(bf16[128,2,64,64]{0,3,2,1:T(8,128)(2,1)} %param.10) | data formatting | bytes 4194304 | tf_op args[0]
  16.2 6.6 %copy.57 = bf16[128,2,64,64]{3,2,1,0:T(8,128)(2,1)} copy(bf16[128,2,64,64]{0,3,2,1:T(8,128)(2,1)S(1)} %copy-done.1) | data formatting | bytes 4194304 | tf_op args[1]
  22.8 3.1 gather_fusion
  25.9 4.3 gather_fusion.1
  30.3 4.2 fusion
  34.5 2.5 fusion.1
  36.9 2.0 fusion.44
  38.9 2.0 fusion.49
  41.0 4.4 add_bitcast_fusion
  45.4 4.2 subtract_bitcast_fusion
  49.5 7.4 %copy.75 = f32[64,2,64,64]{0,1,3,2:T(2,128)} copy(f32[64,2,64,64]{3,2,1,0:T(8,128)} %subtract_bitcast_fusion) | data formatting | bytes 4194304 | tf_op jit(solution)/shard_map/stack | solution.py:36
  56.9 7.4 %copy.74 = f32[64,2,64,64]{0,1,3,2:T(2,128)} copy(f32[64,2,64,64]{3,2,1,0:T(8,128)} %add_bitcast_fusion) | data formatting | bytes 4194304 | tf_op jit(solution)/shard_map/stack | solution.py:36
  64.3 8.5 %fusion.114 = f32[4096,2,2,64]{3,2,1,0:T(2,128)} fusion(f32[1,64,2,4096]{1,2,0,3:T(2,128)} %bitcast.117, f32[1,64,2,4096]{1,2,0,3:T(2,128)} %bitcast.118), kind=kLoop, calls=%fused_computation.122 | loop fusion | flops 1048576 | bytes 8388608
  72.9 12.0 %reshape.77 = f32[32,1,32768]{2,1,0:T(1,128)} reshape(f32[4096,2,2,64]{3,2,1,0:T(2,128)} %fusion.114) | data formatting | bytes 8388608
  84.9 9.2 %all-to-all-start = ((f32[32,1,32768]{2,1,0:T(1,128)}), f32[32,1,32768]{2,1,0:T(1,128)}, u32[]{:S(2)}, u32[]{:S(2)}) async-start(f32[32,1,32768]{2,1,0:T(1,128)} %reshape.77), calls=%async_computation | async-start | bytes 8388608 | tf_op jit(solution)/shard_map/all_to_all | solution.py:71
  94.1 93.8 %all-to-all-done = f32[32,1,32768]{2,1,0:T(1,128)} async-done(((f32[32,1,32768]{2,1,0:T(1,128)}), f32[32,1,32768]{2,1,0:T(1,128)}, u32[]{:S(2)}, u32[]{:S(2)}) %all-to-all-start) | async-done | bytes 4194336 | tf_op jit(solution)/shard_map/all_to_all | solution.py:71
  188.4 13.7 %reduce = f32[32,32768]{1,0:T(8,128)} reduce(f32[32,1,32768]{2,1,0:T(1,128)} %all-to-all-done, f32[]{:T(128)} %broadcast.123), dimensions={1}, to_apply=%all_to_all.11.reduce_sub_computation | reduce | bytes 8388612 | tf_op jit(solution)/shard_map/all_to_all | solution.py:71
  202.2 9.2 %reshape.78 = f32[4096,2,2,64]{3,2,1,0:T(2,128)} reshape(f32[32,32768]{1,0:T(8,128)} %reduce) | data formatting | bytes 8388608
  211.4 12.3 %copy.62 = f32[2,64,2,32,128]{4,2,3,1,0:T(2,128)} copy(f32[2,64,2,32,128]{1,2,0,4,3:T(2,128)} %bitcast.111) | data formatting | bytes 8388608 | tf_op jit(solution)/shard_map/all_to_all | solution.py:71
  223.6 2.5 fusion.113
  228.5 1.2 subtract_bitcast_fusion.1
  229.8 2.6 add_bitcast_fusion.1
  232.4 3.8 copy.76
  236.2 2.8 copy.77
  239.0 8.4 %gather_fusion.2 = f32[3840,64]{1,0:T(8,128)S(1)} fusion(f32[64,8192]{0,1:T(8,128)} %bitcast.110, s32[4096]{0:T(1024)S(1)} %pad_clamp_fusion), kind=kCustom, calls=%fused_computation.1.clone | custom fusion | bytes 1981440 | tf_op jit(solution)/shard_map/jit(_take)/gather | solution.py:50
  247.4 10.1 %gather_fusion.3 = f32[3840,64]{1,0:T(8,128)} fusion(f32[64,8192]{0,1:T(8,128)} %bitcast.109, s32[4096]{0:T(1024)S(1)} %pad_clamp_fusion), kind=kCustom, calls=%fused_computation.3.clone | custom fusion | bytes 1981440 | tf_op jit(solution)/shard_map/jit(_take)/gather | solution.py:51
  257.5 3.5 fusion.36
  261.5 2.6 copy.65
  264.2 163.8 %all-gather.2.cloned.1.call-done = bf16[2,512,3840]{2,0,1:T(2,128)(2,1)} async-done(((bf16[2,64,3840]{2,0,1:T(2,128)(2,1)}), bf16[2,512,3840]{2,0,1:T(2,128)(2,1)}) %all-gather.2.cloned.1.call-update) | async-done | bytes 7864336 | tf_op jit(solution)/shard_map/all_gather | solution.py:75
  428.0 15.5 %fusion.112 = (bf16[1,512,3840]{2,0,1:T(2,128)(2,1)S(1)}, bf16[1,512,3840]{2,0,1:T(2,128)(2,1)S(1)}) fusion(bf16[2,512,3840]{2,0,1:T(2,128)(2,1)} %all-gather.2.cloned.1.call-done), kind=kLoop, calls=%fused_computation.120 | loop fusion | bytes 15728640 | tf_op jit(solution)/shard_map/slice | solution.py:57
  445.8 1.2 fusion.27
  449.3 141.0 %reduce-scatter.2.cloned.1.call-done = f32[2,16,256]{2,1,0:T(8,128)} async-done(((f32[2,512,256]{2,1,0:T(8,128)}), f32[2,16,256]{2,1,0:T(8,128)}) %reduce-scatter.2.cloned.1.call-update) | async-done | bytes 32784 | tf_op jit(solution)/shard_map/reduce_scatter | solution.py:76
  (28 shorter events, 10.2 us)
Async XLA Ops:
  6.5 9.6 %copy-start.1 = (bf16[128,2,64,64]{0,3,2,1:T(8,128)(2,1)S(1)}, bf16[128,2,64,64]{0,3,2,1:T(8,128)(2,1)}, u32[]{:S(2)}) copy-start(bf16[128,2,64,64]{0,3,2,1:T(8,128)(2,1)} %param.11) | copy-start | bytes 6291460
  30.3 4.2 copy-start
  84.9 9.2 %copy-start.2 = (s32[3840]{0:T(1024)S(1)}, s32[3840]{0:T(1024)}, u32[]{:S(2)}) copy-start(s32[3840]{0:T(1024)} %param.14) | copy-start | bytes 46084
  84.9 103.1 %all-to-all-start = ((f32[32,1,32768]{2,1,0:T(1,128)}), f32[32,1,32768]{2,1,0:T(1,128)}, u32[]{:S(2)}, u32[]{:S(2)}) async-start(f32[32,1,32768]{2,1,0:T(1,128)} %reshape.77), calls=%async_computation | async-start | bytes 8388608 | tf_op jit(solution)/shard_map/all_to_all | solution.py:71
  94.0 333.9 %all-gather.2.cloned.1.call-start = ((), (), s32[]{:S(2)}) async-start(), calls=%async_computation.2 | async-start | bytes 8847360 | tf_op jit(solution)/shard_map/all_gather | solution.py:75
  264.1 326.1 %reduce-scatter.2.cloned.1.call-start = ((), (), s32[]{:S(2)}) async-start(), calls=%async_computation.3 | async-start | bytes 1081344 | tf_op jit(solution)/shard_map/reduce_scatter | solution.py:76
  427.9 15.5 %copy-start.3 = (bf16[2,3840,256]{2,1,0:T(8,128)(2,1)S(1)}, bf16[2,3840,256]{2,1,0:T(8,128)(2,1)}, u32[]{:S(2)}) copy-start(bf16[2,3840,256]{2,1,0:T(8,128)(2,1)} %param.15) | copy-start | bytes 11796484
Sparse Core Ops, SparseCore 0:
  264.2 163.6 all-gather.1
  449.4 140.8 reduce-scatter.1
where the time goes:
time: 607 us; the launch traced here: 598 us
  waiting for transfers between devices  399 us (66%)
  local copies, waits for them, and re-layouts  116 us (19%)
  matrix products  30.2 us (5%)
  other arithmetic  29.4 us (5%)
  between operations  14.1 us (2%)
  starting transfers between devices  9.26 us (2%)
    all_gather x1, waiting for transfers between devices, shards(): lax.all_gather(spectra, 'band', axis=1, tiled=True)  164 us
    reduce_scatter x1, waiting for transfers between devices, shards(): lax.psum_scatter(partial_sums, 'grid', scatter_dimension=1, tiled=True)  141 us
    all_to_all x1, waiting for transfers between devices, shards(): lax.all_to_all(planes(density), 'grid', split_axis=3, concat_axis=2, tile...  93.8 us
    unnamed x12, local copies, waits for them, and re-layouts  35.3 us
    slice x1, local copies, waits for them, and re-layouts, project(): spectra[1]  15.5 us
    another operation x2, local copies, waits for them, and re-layouts, planes(): return jnp.stack([real_y, imag_y]).reshape(2, count, slab, rows_y * rows_z)  14.8 us
    all_to_all x1, other arithmetic, shards(): lax.all_to_all(planes(density), 'grid', split_axis=3, concat_axis=2, tile...  13.7 us
    all_to_all x2, local copies, waits for them, and re-layouts, shards(): lax.all_to_all(planes(density), 'grid', split_axis=3, concat_axis=2, tile...  12.8 us
  transfers between devices with their start and end apart: 3, of which 3 were waited for; matrix products, arithmetic and copies ran while one was open for 0% of the time, Pallas kernels for 0%

commit v1 on v0

v1 whole, which is shorter than its diff:
```python
import functools
import math

import jax
import jax.numpy as jnp
import ml_dtypes
import numpy as np
from jax import lax
from jax.experimental import pallas as pl
from jax.experimental.pallas import tpu as pltpu
from jax.sharding import PartitionSpec as P

N = 64
LANES = 128
PAIRS = 64
STRIPS = 32
BANDS = 8
CELLS = 8192
G = 3840
EIG = 256
CHUNKS = 4
ROWS = G // CHUNKS
MESH = pl.DeviceIdType.MESH
F32 = jnp.float32
BF16 = jnp.bfloat16
VMEM_LIMIT = 56 * 1024 * 1024
HALF = math.sqrt(0.5)


def cadd(a, b):
    return (a[0] + b[0], a[1] + b[1])


def csub(a, b):
    return (a[0] - b[0], a[1] - b[1])


def turn(a, k, length):
    k = k % length
    if k == 0:
        return a
    if 4 * k == length:
        return (a[1], -a[0])
    if 2 * k == length:
        return (-a[0], -a[1])
    if 4 * k == 3 * length:
        return (-a[1], a[0])
    if 8 * k == length:
        return ((a[0] + a[1]) * HALF, (a[1] - a[0]) * HALF)
    if 8 * k == 3 * length:
        return ((a[1] - a[0]) * HALF, (a[0] + a[1]) * (-HALF))
    c, s = math.cos(2 * math.pi * k / length), math.sin(2 * math.pi * k / length)
    return (a[0] * c + a[1] * s, a[1] * c - a[0] * s)


def fft4(x):
    a, b, c, d = cadd(x[0], x[2]), csub(x[0], x[2]), cadd(x[1], x[3]), csub(x[1], x[3])
    return [cadd(a, c), (b[0] + d[1], b[1] - d[0]), csub(a, c), (b[0] - d[1], b[1] + d[0])]


def fft8(x):
    even, odd = fft4(x[0::2]), fft4(x[1::2])
    odd = [turn(odd[k], k, 8) for k in range(4)]
    return [cadd(even[k], odd[k]) for k in range(4)] + [csub(even[k], odd[k]) for k in range(4)]


def rfft8(x):
    def four(v):
        a, b, c, d = v[0] + v[2], v[0] - v[2], v[1] + v[3], v[1] - v[3]
        return a + c, (b, -d), a - c

    e0, e1, e2 = four(x[0::2])
    o0, o1, o2 = four(x[1::2])
    o1 = turn(o1, 1, 8)
    low = csub(e1, o1)
    return [e0 + o0, cadd(e1, o1), (e2, -o2), (low[0], -low[1]), e0 - o0]


def z_tables():
    index = np.arange(N)
    angle = (index[:, None] * index[None, :] % N) * (2 * np.pi / N)
    c, s = np.cos(angle) / 512.0, np.sin(angle) / 512.0
    table = np.block([[c, s], [-s, c], [c, -s], [-s, -c]]).astype(np.float32)
    high = table.astype(ml_dtypes.bfloat16)
    low = (table - high.astype(np.float32)).astype(ml_dtypes.bfloat16)
    return np.concatenate([high, high], axis=1), low


def split(value):
    high = value.astype(BF16)
    return high, (value - high.astype(F32)).astype(BF16)


def dot(a, b):
    return jnp.dot(a, b, preferred_element_type=F32)


def one_hot(pairs_ref):
    row = pairs_ref[...]
    row = jnp.concatenate([row, row], axis=1)
    r = lax.broadcasted_iota(jnp.int32, (2 * LANES, LANES), 0)
    lane = lax.broadcasted_iota(jnp.int32, (2 * LANES, LANES), 1)
    hit = (r % LANES == row) & (r // LANES == lane // PAIRS)
    return jnp.where(hit, 1.0, 0.0).astype(BF16)


def density(occ_ref, emp_ref, pocc_ref, pemp_ref, dens):
    pick_occ, pick_emp = one_hot(pocc_ref), one_hot(pemp_ref)
    rows = 512

    @pl.loop(0, N * N // rows)
    def _(step):
        at = pl.ds(pl.multiple_of(step * rows, rows), rows)
        occ = jnp.concatenate([occ_ref[0, at, :], occ_ref[1, at, :]], axis=1)
        emp = jnp.concatenate([emp_ref[0, at, :], emp_ref[1, at, :]], axis=1)
        dens[at, :] = dot(occ, pick_occ) * dot(emp, pick_emp)


def transform_y(dens, spec, work):
    @pl.loop(0, 8)
    def _(tile):
        at = pl.multiple_of(tile * 8, 8)
        for n2 in range(8):
            outs = rfft8([dens[pl.ds((8 * n1 + n2) * N + at, 8), :] for n1 in range(8)])
            work[0, n2, 0] = outs[0]
            for k1 in (1, 2, 3):
                re, im = turn(outs[k1], n2 * k1, 64)
                work[k1, n2, 0] = re
                work[k1, n2, 1] = im
            angle = 2 * math.pi * n2 * 4 / 64
            work[4, n2, 0] = outs[4] * math.cos(angle)
            work[4, n2, 1] = outs[4] * (-math.sin(angle))
        outs = rfft8([work[0, n2, 0] for n2 in range(8)])
        zero = jnp.zeros_like(outs[0])
        for k2 in range(5):
            re, im = (outs[k2], zero) if k2 in (0, 4) else outs[k2]
            spec[8 * k2, pl.ds(at, 8), :] = re
            spec[8 * k2, pl.ds(N + at, 8), :] = im
        for k1 in (1, 2, 3, 4):
            outs = fft8([(work[k1, n2, 0], work[k1, n2, 1]) for n2 in range(8)])
            for k2 in range(8 if k1 < 4 else 4):
                ky = k1 + 8 * k2
                re, im = outs[k2]
                if ky > 32:
                    ky, im = 64 - ky, -im
                spec[ky, pl.ds(at, 8), :] = re
                spec[ky, pl.ds(N + at, 8), :] = im


def planes_kernel(
    pocc_ref, pemp_ref, occ_ref, emp_ref, t1_ref, t2_ref, recv,
    dens, spec, work, send, send_sems, recv_sems, local_sem,
):
    band = lax.axis_index("band")
    me = lax.axis_index("grid")
    barrier = pltpu.get_barrier_semaphore()

    @pl.loop(1, STRIPS)
    def _(k):
        pl.semaphore_signal(barrier, inc=1, device_id=(band, (me + k) % STRIPS), device_id_type=MESH)

    density(occ_ref, emp_ref, pocc_ref, pemp_ref, dens)
    transform_y(dens, spec, work)
    pl.semaphore_wait(barrier, STRIPS - 1)

    def copy(strip):
        return pltpu.make_async_remote_copy(
            src_ref=send.at[strip], dst_ref=recv.at[me], send_sem=send_sems.at[strip],
            recv_sem=recv_sems.at[me], device_id=(band, strip), device_id_type=MESH,
        )

    def start(strip):
        @pl.when(strip != me)
        def _():
            copy(strip).start()

    @pl.loop(0, 16)
    def _(step):
        j = (me + step) % 16
        h0, l0 = split(spec[2 * j])
        h1, l1 = split(spec[2 * j + 1])
        high = jnp.concatenate([h0, h1], axis=1)
        low = jnp.concatenate([l0, l1], axis=1)
        out = dot(t1_ref[...], jnp.concatenate([high, low], axis=0)) + dot(t2_ref[...], high)
        out = out.astype(BF16)
        send[j, 0] = out[:LANES, :LANES]
        send[j, 1] = out[:LANES, LANES:]
        start(j)

        @pl.when(j > 0)
        def _():
            send[32 - j, 0] = out[LANES:, :LANES]

        send[31 - j, 1] = out[LANES:, LANES:]

    h0, l0 = split(spec[32])
    out = dot(t1_ref[:LANES, :], jnp.concatenate([h0, l0], axis=0)) + dot(t2_ref[:LANES, :], h0)
    send[16, 0] = out.astype(BF16)

    @pl.loop(0, 16)
    def _(step):
        start(16 + (me + step) % 16)

    own = pltpu.make_async_copy(send.at[me], recv.at[me], local_sem)
    own.start()
    own.wait()

    @pl.loop(1, STRIPS)
    def _(k):
        other = (me + k) % STRIPS
        copy(other).wait_send()
        pltpu.make_async_remote_copy(
            src_ref=send.at[other], dst_ref=recv.at[other], send_sem=send_sems.at[other],
            recv_sem=recv_sems.at[other], device_id=(band, other), device_id_type=MESH,
        ).wait_recv()


def planes(pocc, pemp, occ, emp):
    t1, t2 = z_tables()
    vmem = pl.BlockSpec(memory_space=pltpu.VMEM)
    return pl.pallas_call(
        planes_kernel,
        out_shape=jax.ShapeDtypeStruct((STRIPS, 2, 2 * N, LANES), BF16),
        in_specs=[vmem] * 6,
        out_specs=pl.BlockSpec(memory_space=pl.ANY),
        scratch_shapes=[
            pltpu.VMEM((N * N, LANES), F32),
            pltpu.VMEM((33, 2 * N, LANES), F32),
            pltpu.VMEM((5, 8, 2, 8, LANES), F32),
            pltpu.VMEM((STRIPS, 2, 2 * N, LANES), BF16),
            pltpu.SemaphoreType.DMA((STRIPS,)),
            pltpu.SemaphoreType.DMA((STRIPS,)),
            pltpu.SemaphoreType.DMA,
        ],
        compiler_params=pltpu.CompilerParams(
            collective_id=0, has_side_effects=True, vmem_limit_bytes=VMEM_LIMIT
        ),
        name="planes",
    )(pocc, pemp, occ, emp, jnp.asarray(t1), jnp.asarray(t2))


def transform_x(recv, cells, work):
    lane = lax.broadcasted_iota(jnp.int32, (8, LANES), 1)
    left = lane < PAIRS

    @pl.loop(0, 2 * 4)
    def _(tile):
        kyl = tile // 4
        at = pl.multiple_of((tile % 4) * 16, 16)
        for n2 in range(8):
            outs = fft4(
                [
                    (
                        recv[8 * n1 + n2, kyl, pl.ds(at, 16), :].astype(F32),
                        recv[8 * n1 + n2, kyl, pl.ds(N + at, 16), :].astype(F32),
                    )
                    for n1 in range(4)
                ]
            )
            for k1 in range(4):
                re, im = turn(outs[k1], n2 * k1, 32)
                work[k1, n2, 0] = re
                work[k1, n2, 1] = im
        for half in range(2):
            rows = slice(8 * half, 8 * half + 8)
            for k1 in range(4):
                outs = fft8([(work[k1, n2, 0, rows], work[k1, n2, 1, rows]) for n2 in range(8)])
                for k2 in range(8):
                    kx = k1 + 4 * k2
                    re, im = outs[k2]
                    c = jnp.where(left, 1.0, math.cos(2 * math.pi * kx / 64))
                    s = jnp.where(left, 0.0, math.sin(2 * math.pi * kx / 64))
                    re, im = re * c + im * s, im * c - re * s
                    even = jnp.where(left, re, pltpu.roll(im, PAIRS, axis=1))
                    odd = jnp.where(left, pltpu.roll(re, PAIRS, axis=1), im)
                    cell = kyl * N + at + 8 * half
                    cells[pl.ds(kx * LANES + cell, 8), :] = even + odd
                    cells[pl.ds((kx + 32) * LANES + cell, 8), :] = even - odd


def pick(cell_ref, cells, rows, out):
    block = 16

    @pl.loop(0, G // block)
    def _(step):
        at = pl.multiple_of(step * block, block)
        for i in range(block):
            rows[pl.ds(at + i, 1), :] = cells[pl.ds(cell_ref[at + i], 1), :]

    @pl.loop(0, G // 128)
    def _(step):
        at = pl.ds(pl.multiple_of(step * 128, 128), 128)
        out[at, :] = rows[at, :].astype(BF16)


def columns_kernel(cell_ref, recv, out, cells, work, rows):
    transform_x(recv, cells, work)
    pick(cell_ref, cells, rows, out)


def columns(g_cell, recv):
    vmem = pl.BlockSpec(memory_space=pltpu.VMEM)
    return pl.pallas_call(
        columns_kernel,
        out_shape=jax.ShapeDtypeStruct((G, LANES), BF16),
        in_specs=[pl.BlockSpec(memory_space=pltpu.SMEM), vmem],
        out_specs=vmem,
        scratch_shapes=[
            pltpu.VMEM((CELLS, LANES), F32),
            pltpu.VMEM((4, 8, 2, 16, LANES), F32),
            pltpu.VMEM((G, LANES), F32),
        ],
        compiler_params=pltpu.CompilerParams(vmem_limit_bytes=VMEM_LIMIT),
        name="columns",
    )(g_cell, recv)


def project_kernel(
    spectra, eig, out, held, sums, parts, z_send, z_recv, x_send, x_recv, f_send, f_recv, r_send, r_recv,
):
    band = lax.axis_index("band")
    me = lax.axis_index("grid")
    right, left, opposite = (band + 2) % BANDS, (band + 6) % BANDS, (band + 4) % BANDS

    def other(b):
        return b + 1 - 2 * (b % 2)

    partner = other(band)
    barrier = pltpu.get_barrier_semaphore()
    for b in (right, left, partner):
        pl.semaphore_signal(barrier, inc=1, device_id=(b, me), device_id_type=MESH)

    @pl.loop(1, STRIPS)
    def _(k):
        pl.semaphore_signal(barrier, inc=1, device_id=(band, (me + k) % STRIPS), device_id_type=MESH)

    pl.semaphore_wait(barrier, STRIPS + 2)

    def at(c):
        return pl.ds(c * ROWS, ROWS)

    def move(src, block, c, send_sem, recv_sem, to):
        return pltpu.make_async_remote_copy(
            src_ref=src, dst_ref=held.at[block, at(c)], send_sem=send_sem, recv_sem=recv_sem,
            device_id=(to, me), device_id_type=MESH,
        )

    def z_copy(c):
        return move(spectra.at[at(c)], band, c, z_send.at[c], z_recv.at[c], partner)

    def x_copy(kind, side, c):
        src = spectra.at[at(c)] if kind == 0 else held.at[partner, at(c)]
        return move(
            src, partner if kind else band, c, x_send.at[kind, side, c], x_recv.at[kind, side, c],
            left if side else right,
        )

    def f_copy(kind, c):
        side = 0 if c < CHUNKS // 2 else 1
        block = right if side else left
        if kind:
            block = other(block)
        return move(
            held.at[block, at(c)], block, c, f_send.at[kind, c], f_recv.at[kind, c],
            left if side else right,
        )

    def multiply(src, block):
        def body(c, acc):
            rows = pl.ds(pl.multiple_of(c * 480, 480), 480)
            s = src[rows, :]
            dims = (((0,), (0,)), ((), ()))
            return (
                acc[0] + lax.dot_general(s, eig[0, rows, :], dims, preferred_element_type=F32),
                acc[1] + lax.dot_general(s, eig[1, rows, :], dims, preferred_element_type=F32),
            )

        zero = jnp.zeros((2 * PAIRS, EIG), F32)
        p0, p1 = lax.fori_loop(0, G // 480, body, (zero, zero))
        sums[block, :, :EIG] = p0[:PAIRS] + p1[PAIRS:]
        sums[block, :, EIG:] = p1[:PAIRS] - p0[PAIRS:]
        for i in range(4):
            strip = block * 4 + i

            @pl.when(strip != me)
            def _():
                r_copy(strip).start()

    def r_copy(strip):
        rows = pl.ds(pl.multiple_of((strip % 4) * 16, 16), 16)
        return pltpu.make_async_remote_copy(
            src_ref=sums.at[strip // 4, rows], dst_ref=parts.at[me], send_sem=r_send.at[strip],
            recv_sem=r_recv.at[me], device_id=(band, strip), device_id_type=MESH,
        )

    for c in range(CHUNKS):
        z_copy(c).start()
        x_copy(0, 0, c).start()
        x_copy(0, 1, c).start()

    def arrive(kind, c):
        x_copy(kind, 0, c).wait_recv()
        x_copy(kind, 1, c).wait_recv()
        f_copy(kind, c).start()

    multiply(spectra, band)
    for c in range(CHUNKS):
        arrive(0, c)
        z_copy(c).wait_recv()
        x_copy(1, 0, c).start()
        x_copy(1, 1, c).start()
    multiply(held.at[left], left)
    multiply(held.at[right], right)
    multiply(held.at[partner], partner)
    for c in range(CHUNKS):
        f_copy(0, c).wait_recv()
        arrive(1, c)
    multiply(held.at[opposite], opposite)
    multiply(held.at[other(left)], other(left))
    multiply(held.at[other(right)], other(right))
    for c in range(CHUNKS):
        f_copy(1, c).wait_recv()
    multiply(held.at[other(opposite)], other(opposite))

    own = pl.ds(pl.multiple_of((me % 4) * 16, 16), 16)

    def add(k, total):
        src = (me + k) % STRIPS
        pltpu.make_async_remote_copy(
            src_ref=parts.at[src], dst_ref=parts.at[src], send_sem=r_send.at[src],
            recv_sem=r_recv.at[src], device_id=(band, src), device_id_type=MESH,
        ).wait_recv()
        return total + parts[src]

    total = lax.fori_loop(1, STRIPS, add, sums[me // 4, own, :])
    out[0] = total[:, :EIG]
    out[1] = total[:, EIG:]

    for c in range(CHUNKS):
        z_copy(c).wait_send()
        for kind in range(2):
            f_copy(kind, c).wait_send()
            for side in range(2):
                x_copy(kind, side, c).wait_send()

    @pl.loop(1, STRIPS)
    def _(k):
        r_copy((me + k) % STRIPS).wait_send()


def project(spectra, eigvecs):
    vmem = pl.BlockSpec(memory_space=pltpu.VMEM)
    return pl.pallas_call(
        project_kernel,
        out_shape=jax.ShapeDtypeStruct((2, 16, EIG), F32),
        in_specs=[vmem, vmem],
        out_specs=vmem,
        scratch_shapes=[
            pltpu.VMEM((BANDS, G, LANES), BF16),
            pltpu.VMEM((BANDS, PAIRS, 2 * EIG), F32),
            pltpu.VMEM((STRIPS, 16, 2 * EIG), F32),
            pltpu.SemaphoreType.DMA((CHUNKS,)),
            pltpu.SemaphoreType.DMA((CHUNKS,)),
            pltpu.SemaphoreType.DMA((2, 2, CHUNKS)),
            pltpu.SemaphoreType.DMA((2, 2, CHUNKS)),
            pltpu.SemaphoreType.DMA((2, CHUNKS)),
            pltpu.SemaphoreType.DMA((2, CHUNKS)),
            pltpu.SemaphoreType.DMA((STRIPS,)),
            pltpu.SemaphoreType.DMA((STRIPS,)),
        ],
        compiler_params=pltpu.CompilerParams(
            collective_id=1, has_side_effects=True, vmem_limit_bytes=VMEM_LIMIT
        ),
        name="project",
    )(spectra, eigvecs)


def shards(occupied, empty, pair_occ, pair_emp, g_cell, eigvecs):
    occ = jnp.transpose(occupied, (1, 2, 3, 0)).reshape(2, N * N, LANES)
    emp = jnp.transpose(empty, (1, 2, 3, 0)).reshape(2, N * N, LANES)
    recv = planes(pair_occ.reshape(1, PAIRS), pair_emp.reshape(1, PAIRS), occ, emp)
    spectra = columns(g_cell, recv)
    return project(spectra, eigvecs)


def solution(mesh):
    in_specs = (
        P(None, "grid", None, None),
        P(None, "grid", None, None),
        P("band"),
        P("band"),
        P("grid"),
        P(None, "grid", "band"),
    )
    out_specs = P(None, "grid", "band")
    return jax.shard_map(shards, mesh=mesh, in_specs=in_specs, out_specs=out_specs, check_vma=False)
```

time: 607 us -> 168 us (0.28)
  the two profiles are of different devices: /device:TPU:2 before, /device:TPU:55 now
where the time goes in v1:
time: 168 us
  Pallas kernels  166 us (99%)
    pallas_call x1, Pallas kernels, project(): pl.pallas_call(project_kernel, out_shape=jax.ShapeDtypeStruct((2, 16, EIG...  100 us
    pallas_call x1, Pallas kernels, planes(): pl.pallas_call(planes_kernel, out_shape=jax.ShapeDtypeStruct((STRIPS, 2,...  56.1 us
    pallas_call x1, Pallas kernels, columns(): pl.pallas_call(columns_kernel, out_shape=jax.ShapeDtypeStruct((G, LANES),...  9.6 us

profile of v1, /device:TPU:55, one launch (start us, length us, event | category | flops | bytes accessed | tf_op | source)
XLA Modules:
  0.0 167.6 jit_solution(6602625529514687974)
XLA Ops:
  0.0 56.1 %planes.1.recv = bf16[32,2,128,128]{3,2,1,0:T(8,128)(2,1)} custom-call(s32[1,64]{1,0:T(1,128)} %bitcast.10, s32[1,64]{1,0:T(1,128)} %bitcast.11, bf16[2,4096,128]{2,1,0:T(8,128)(2,1)} %bitcast.8, bf16[2,4096,128]{2,1,0:T(8,128)(2,1)} %bitcast.9, bf16[256,256]{1,0:T(8,128)(2,1)} %constant.4.clone.t1_ref, bf16[256,128]{1,0:T(8,128)(2,1)} %constant.5.clone.t2_ref), custom_call_target="tpu_custom_call" | custom-call | tf_op jit(solution)/shard_map/planes/pallas_call | solution.py:221
  56.1 9.6 %columns.1.spectra = bf16[3840,128]{1,0:T(8,128)(2,1)} custom-call(s32[3840]{0:T(1024)} %cell_ref.1, bf16[32,2,128,128]{3,2,1,0:T(8,128)(2,1)} %planes.1.recv), custom_call_target="tpu_custom_call" | custom-call | tf_op jit(solution)/shard_map/columns/pallas_call | solution.py:303
  65.7 100.5 %project.1 = f32[2,16,256]{2,1,0:T(8,128)} custom-call(bf16[3840,128]{1,0:T(8,128)(2,1)} %columns.1.spectra, bf16[2,3840,256]{2,1,0:T(8,128)(2,1)} %eig.1), custom_call_target="tpu_custom_call" | custom-call | tf_op jit(solution)/shard_map/project/pallas_call | solution.py:453
  166.2 1.4 copy.10

commit v2 on v0

v2 whole, which is shorter than its diff:
```python
import math

import jax
import jax.numpy as jnp
import ml_dtypes
import numpy as np
from jax import lax
from jax.experimental import pallas as pl
from jax.experimental.pallas import tpu as pltpu
from jax.sharding import PartitionSpec as P

N = 64
LANES = 128
PAIRS = 64
STRIPS = 32
BANDS = 8
CELLS = 8192
G = 3840
EIG = 256
ROWS = G // 2
XS = 4
SETS = 2
MESH = pl.DeviceIdType.MESH
F32 = jnp.float32
BF16 = jnp.bfloat16
VMEM_LIMIT = 56 * 1024 * 1024
HALF = math.sqrt(0.5)


def cadd(a, b):
    return (a[0] + b[0], a[1] + b[1])


def csub(a, b):
    return (a[0] - b[0], a[1] - b[1])


def turn(a, k, length):
    k = k % length
    if k == 0:
        return a
    if 4 * k == length:
        return (a[1], -a[0])
    if 2 * k == length:
        return (-a[0], -a[1])
    if 4 * k == 3 * length:
        return (-a[1], a[0])
    if 8 * k == length:
        return ((a[0] + a[1]) * HALF, (a[1] - a[0]) * HALF)
    if 8 * k == 3 * length:
        return ((a[1] - a[0]) * HALF, (a[0] + a[1]) * (-HALF))
    c, s = math.cos(2 * math.pi * k / length), math.sin(2 * math.pi * k / length)
    return (a[0] * c + a[1] * s, a[1] * c - a[0] * s)


def fft4(x):
    a, b, c, d = cadd(x[0], x[2]), csub(x[0], x[2]), cadd(x[1], x[3]), csub(x[1], x[3])
    return [cadd(a, c), (b[0] + d[1], b[1] - d[0]), csub(a, c), (b[0] - d[1], b[1] + d[0])]


def fft8(x):
    even, odd = fft4(x[0::2]), fft4(x[1::2])
    odd = [turn(odd[k], k, 8) for k in range(4)]
    return [cadd(even[k], odd[k]) for k in range(4)] + [csub(even[k], odd[k]) for k in range(4)]


def rfft8(x):
    def four(v):
        a, b, c, d = v[0] + v[2], v[0] - v[2], v[1] + v[3], v[1] - v[3]
        return a + c, (b, -d), a - c

    e0, e1, e2 = four(x[0::2])
    o0, o1, o2 = four(x[1::2])
    o1 = turn(o1, 1, 8)
    low = csub(e1, o1)
    return [e0 + o0, cadd(e1, o1), (e2, -o2), (low[0], -low[1]), e0 - o0]


def z_tables():
    index = np.arange(N)
    angle = (index[:, None] * index[None, :] % N) * (2 * np.pi / N)
    c, s = np.cos(angle) / 512.0, np.sin(angle) / 512.0
    table = np.block([[c, s], [-s, c], [c, -s], [-s, -c]]).astype(np.float32)
    high = table.astype(ml_dtypes.bfloat16)
    low = (table - high.astype(np.float32)).astype(ml_dtypes.bfloat16)
    return np.concatenate([high, high], axis=1), low


def split(value):
    high = value.astype(BF16)
    return high, (value - high.astype(F32)).astype(BF16)


def dot(a, b):
    return jnp.dot(a, b, preferred_element_type=F32)


def one_hot(row):
    r = lax.broadcasted_iota(jnp.int32, (2 * LANES, LANES), 0)
    lane = lax.broadcasted_iota(jnp.int32, (2 * LANES, LANES), 1)
    hit = (r % LANES == row) & (r // LANES == lane // PAIRS)
    return jnp.where(hit, 1.0, 0.0).astype(BF16)


def density(occ_ref, emp_ref, pairs, dens):
    pick_occ, pick_emp = one_hot(pairs[0:1, :]), one_hot(pairs[1:2, :])
    rows = 512

    @pl.loop(0, N * N // rows)
    def _(step):
        at = pl.ds(pl.multiple_of(step * rows, rows), rows)
        occ = jnp.concatenate([occ_ref[0, at, :], occ_ref[1, at, :]], axis=1)
        emp = jnp.concatenate([emp_ref[0, at, :], emp_ref[1, at, :]], axis=1)
        dens[at, :] = dot(occ, pick_occ) * dot(emp, pick_emp)


def transform_y(dens, spec, work):
    @pl.loop(0, 8)
    def _(tile):
        at = pl.multiple_of(tile * 8, 8)
        for n2 in range(8):
            outs = rfft8([dens[pl.ds((8 * n1 + n2) * N + at, 8), :] for n1 in range(8)])
            work[0, n2, 0] = outs[0]
            for k1 in (1, 2, 3):
                re, im = turn(outs[k1], n2 * k1, 64)
                work[k1, n2, 0] = re
                work[k1, n2, 1] = im
            angle = 2 * math.pi * n2 * 4 / 64
            work[4, n2, 0] = outs[4] * math.cos(angle)
            work[4, n2, 1] = outs[4] * (-math.sin(angle))
        outs = rfft8([work[0, n2, 0] for n2 in range(8)])
        zero = jnp.zeros_like(outs[0])
        for k2 in range(5):
            re, im = (outs[k2], zero) if k2 in (0, 4) else outs[k2]
            spec[8 * k2, pl.ds(at, 8), :] = re
            spec[8 * k2, pl.ds(N + at, 8), :] = im
        for k1 in (1, 2, 3, 4):
            outs = fft8([(work[k1, n2, 0], work[k1, n2, 1]) for n2 in range(8)])
            for k2 in range(8 if k1 < 4 else 4):
                ky = k1 + 8 * k2
                re, im = outs[k2]
                if ky > 32:
                    ky, im = 64 - ky, -im
                spec[ky, pl.ds(at, 8), :] = re
                spec[ky, pl.ds(N + at, 8), :] = im


def transform_x(recv, cells, work):
    lane = lax.broadcasted_iota(jnp.int32, (8, LANES), 1)
    left = lane < PAIRS

    @pl.loop(0, 2 * 4)
    def _(tile):
        kyl = tile // 4
        at = pl.multiple_of((tile % 4) * 16, 16)
        for n2 in range(8):
            outs = fft4(
                [
                    (
                        recv[8 * n1 + n2, kyl, pl.ds(at, 16), :].astype(F32),
                        recv[8 * n1 + n2, kyl, pl.ds(N + at, 16), :].astype(F32),
                    )
                    for n1 in range(4)
                ]
            )
            for k1 in range(4):
                re, im = turn(outs[k1], n2 * k1, 32)
                work[k1, n2, 0] = re
                work[k1, n2, 1] = im
        for half in range(2):
            rows = slice(8 * half, 8 * half + 8)
            for k1 in range(4):
                outs = fft8([(work[k1, n2, 0, rows], work[k1, n2, 1, rows]) for n2 in range(8)])
                for k2 in range(8):
                    kx = k1 + 4 * k2
                    re, im = outs[k2]
                    c = jnp.where(left, 1.0, math.cos(2 * math.pi * kx / 64))
                    s = jnp.where(left, 0.0, math.sin(2 * math.pi * kx / 64))
                    re, im = re * c + im * s, im * c - re * s
                    even = jnp.where(left, re, pltpu.roll(im, PAIRS, axis=1))
                    odd = jnp.where(left, pltpu.roll(re, PAIRS, axis=1), im)
                    cell = kyl * N + at + 8 * half
                    cells[pl.ds(kx * LANES + cell, 8), :] = even + odd
                    cells[pl.ds((kx + 32) * LANES + cell, 8), :] = even - odd


def pick(cell_ref, cells, rows, out):
    block = 16

    @pl.loop(0, G // block)
    def _(step):
        at = pl.multiple_of(step * block, block)
        for i in range(block):
            rows[pl.ds(at + i, 1), :] = cells[pl.ds(cell_ref[at + i], 1), :]

    @pl.loop(0, G // 128)
    def _(step):
        at = pl.ds(pl.multiple_of(step * 128, 128), 128)
        out[at, :] = rows[at, :].astype(BF16)


def kernel(
    cell_ref, pairs_ref, occ_ref, emp_ref, t1_ref, t2_ref, eig_ref, out,
    lists, dens, spec, work_y, send, recv, cells, work_x, rows, own, held, eigs, sums, parts, done, final,
    list_sems, a_send, a_recv, local_sems, e_send, e_recv, x_send, x_recv, r_send, r_recv, f_send, f_recv,
):
    band = lax.axis_index("band")
    me = lax.axis_index("grid")
    x, zh = band // 2, band % 2
    zl, low = me // 8, me % 8
    core = me % 2
    z = zh * 4 + zl
    half = x % 2

    def peer(strip):
        steps = (strip // 8 - zl + 4) % 4
        side = (zl // 2 + core + strip) % 2
        away = steps - 4 * (steps // 3) - 4 * side * (steps // 2 - steps // 3)
        return (2 * x + ((z + away + 8) % 8) // 4, strip)

    def along_x(step):
        return (2 * ((x + step) % XS) + zh, me)

    partner_z = (band + 1 - 2 * zh, me)
    partner_x = (band + 2 - 4 * half, me)

    barrier = pltpu.get_barrier_semaphore()

    def greet(device):
        pl.semaphore_signal(barrier, inc=1, device_id=device, device_id_type=MESH)

    def remote(src, dst, send_sem, recv_sem, device):
        return pltpu.make_async_remote_copy(
            src_ref=src, dst_ref=dst, send_sem=send_sem, recv_sem=recv_sem, device_id=device, device_id_type=MESH
        )

    @pl.loop(1, STRIPS)
    def _(k):
        greet(peer((me + k) % STRIPS))

    greet(partner_z)
    for step in (1, 2, 3):
        greet(along_x(step))

    @pl.loop(0, 16)
    def _(k):
        source = (k // 4) * 8 + 2 * (low % 4) + k % 2
        to = 2 * (2 * (x // 2) + (k // 2) % 2) + zh

        @pl.when(jnp.logical_or(source != me, to != band))
        def _():
            greet((to, source))

    mine = jnp.where(jnp.logical_or(low == 0, low == 7), 1, 0)
    list_own = pltpu.make_async_copy(pairs_ref, lists.at[zh], local_sems.at[0])
    list_own.start()
    eig_own = [
        pltpu.make_async_copy(
            eig_ref.at[i, pl.ds(pl.multiple_of(half * ROWS, ROWS), ROWS)],
            eigs.at[:, pl.ds(pl.multiple_of(half * 2 * EIG + i * EIG, EIG), EIG)],
            local_sems.at[1 + i],
        )
        for i in range(2)
    ]
    for copy in eig_own:
        copy.start()
    list_own.wait()
    pl.semaphore_wait(barrier, 31 + 1 + 3 + 16 - mine)

    list_copy = remote(lists.at[zh], lists.at[zh], list_sems.at[0], list_sems.at[1], partner_z)
    list_copy.start()
    eig_copy = [
        remote(
            eig_ref.at[i, pl.ds(pl.multiple_of((1 - half) * ROWS, ROWS), ROWS)],
            eigs.at[:, pl.ds(pl.multiple_of(half * 2 * EIG + i * EIG, EIG), EIG)],
            e_send.at[i], e_recv.at[i], partner_x,
        )
        for i in range(2)
    ]
    for copy in eig_copy:
        copy.start()
    list_copy.wait()

    def a_copy(which, strip):
        return remote(
            send.at[which, strip], recv.at[which, me], a_send.at[which, strip], a_recv.at[which, me], peer(strip)
        )

    def planes(which):
        density(occ_ref, emp_ref, lists[which], dens)
        transform_y(dens, spec, work_y)

        def start(strip):
            @pl.when(strip != me)
            def _():
                if which:
                    a_copy(0, strip).wait_send()
                a_copy(which, strip).start()

        @pl.loop(0, 16)
        def _(step):
            j = (me + step) % 16
            h0, l0 = split(spec[2 * j])
            h1, l1 = split(spec[2 * j + 1])
            high = jnp.concatenate([h0, h1], axis=1)
            low_part = jnp.concatenate([l0, l1], axis=1)
            both = dot(t1_ref[...], jnp.concatenate([high, low_part], axis=0)) + dot(t2_ref[...], high)
            both = both.astype(BF16)
            send[which, j, 0] = both[:LANES, :LANES]
            send[which, j, 1] = both[:LANES, LANES:]
            start(j)

            @pl.when(j > 0)
            def _():
                send[which, 32 - j, 0] = both[LANES:, :LANES]

            send[which, 31 - j, 1] = both[LANES:, LANES:]

        h0, l0 = split(spec[32])
        one = dot(t1_ref[:LANES, :], jnp.concatenate([h0, l0], axis=0)) + dot(t2_ref[:LANES, :], h0)
        send[which, 16, 0] = one.astype(BF16)

        @pl.loop(0, 16)
        def _(step):
            start(16 + (me + step) % 16)

        copy = pltpu.make_async_copy(send.at[which, me], recv.at[which, me], local_sems.at[3])
        copy.start()
        copy.wait()

    def x_copy(which, step):
        part = half if step == 2 else 1 - half
        return remote(
            own.at[which, pl.ds(pl.multiple_of(part * ROWS, ROWS), ROWS)], held.at[which, x],
            x_send.at[which, step - 1], x_recv.at[which, step - 1], along_x(step),
        )

    def columns(which):
        @pl.loop(1, STRIPS)
        def _(k):
            source = (me + k) % STRIPS
            remote(
                send.at[which, source], recv.at[which, source], a_send.at[which, source],
                a_recv.at[which, source], peer(source),
            ).wait_recv()

        transform_x(recv.at[which], cells, work_x)
        pick(cell_ref, cells, rows, own.at[which])
        for step in (1, 3, 2):
            x_copy(which, step).start()

    def r_copy(block, to):
        return remote(
            sums.at[block, pl.ds(pl.multiple_of(to * 8, 8), 8)], parts.at[low, block],
            r_send.at[block, to], r_recv.at[low, block], (band, zl * 8 + to),
        )

    def multiply(src, block):
        @pl.loop(0, 2)
        def _(q):
            at = pl.multiple_of(q * 2 * EIG, 2 * EIG)
            part = lax.dot_general(
                src[...], eigs[:, pl.ds(at, 2 * EIG)], (((0,), (0,)), ((), ())), preferred_element_type=F32
            )
            sums[block, :, pl.ds(at, EIG)] = part[:PAIRS, :EIG] + part[PAIRS:, EIG:]
            sums[block, :, pl.ds(at + EIG, EIG)] = part[:PAIRS, EIG:] - part[PAIRS:, :EIG]

        @pl.loop(1, 8)
        def _(k):
            r_copy(block, (low + k) % 8).start()

    def multiply_own(which):
        at = pl.ds(pl.multiple_of(half * ROWS, ROWS), ROWS)
        multiply(own.at[which, at], 2 * x + which)

    def multiply_from(which, step):
        x_copy(which, step).wait_recv()
        source = (x - step + XS) % XS
        multiply(held.at[which, source], 2 * source + which)

    def f_copy(block, q):
        owner = (block // 2) * 8 + 4 * (block % 2) + low // 2
        slot = (zl * 2 + half) * 2 + low % 2
        return remote(
            done.at[block, :, pl.ds(q * 2 * EIG, 2 * EIG)], final.at[slot],
            f_send.at[block, q], f_recv.at[slot], (2 * (2 * (x // 2) + q) + zh, owner),
        )

    def here(block, q):
        owner = (block // 2) * 8 + 4 * (block % 2) + low // 2
        return jnp.logical_and(owner == me, half == q)

    def reduce(which):
        @pl.loop(0, XS)
        def _(step):
            block = 2 * ((x + XS - step) % XS) + which
            mine_at = pl.ds(pl.multiple_of(low * 8, 8), 8)

            def add(k, total):
                source = (low + k) % 8
                remote(
                    sums.at[block, mine_at], parts.at[source, block], r_send.at[block, source],
                    r_recv.at[source, block], (band, zl * 8 + source),
                ).wait_recv()
                return total + parts[source, block]

            done[block] = lax.fori_loop(1, 8, add, sums[block, mine_at, :])
            for q in range(2):
                local = here(block, q)

                @pl.when(jnp.logical_not(local))
                def _():
                    f_copy(block, q).start()

                @pl.when(local)
                def _():
                    slot = (zl * 2 + half) * 2 + low % 2
                    final[slot] = done[block, :, q * 2 * EIG : (q + 1) * 2 * EIG]

    planes(0)
    planes(1)
    columns(0)
    for copy in eig_own:
        copy.wait()
    for copy in eig_copy:
        copy.wait_recv()
    multiply_own(0)
    columns(1)
    multiply_own(1)
    for step in (1, 3, 2):
        multiply_from(0, step)
    multiply_from(1, 1)
    multiply_from(1, 3)
    reduce(0)
    multiply_from(1, 2)
    reduce(1)

    for row in range(2):
        total = jnp.zeros((8, 2 * EIG), F32)
        for k in range(8):
            slot = 2 * k + row
            local = jnp.logical_and(
                jnp.logical_and(zl * 2 + half == k, low % 2 == row), jnp.logical_or(low == 0, low == 7)
            )

            @pl.when(jnp.logical_not(local))
            def _():
                remote(
                    final.at[slot], final.at[slot], f_send.at[0, 0], f_recv.at[slot], partner_x
                ).wait_recv()

            total = total + final[slot]
        out[0, 8 * row : 8 * row + 8, :] = total[:, :EIG]
        out[1, 8 * row : 8 * row + 8, :] = total[:, EIG:]

    for copy in eig_copy:
        copy.wait_send()

    @pl.loop(1, STRIPS)
    def _(k):
        a_copy(1, (me + k) % STRIPS).wait_send()

    for which in range(SETS):
        for step in (1, 2, 3):
            x_copy(which, step).wait_send()

    @pl.loop(0, BANDS)
    def _(block):
        @pl.loop(1, 8)
        def _(k):
            r_copy(block, (low + k) % 8).wait_send()

        for q in range(2):
            @pl.when(jnp.logical_not(here(block, q)))
            def _():
                f_copy(block, q).wait_send()


def run(g_cell, pairs, occ, emp, eigvecs):
    t1, t2 = z_tables()
    vmem = pl.BlockSpec(memory_space=pltpu.VMEM)
    anywhere = pl.BlockSpec(memory_space=pl.ANY)
    dma = pltpu.SemaphoreType.DMA
    return pl.pallas_call(
        kernel,
        out_shape=jax.ShapeDtypeStruct((2, 16, EIG), F32),
        in_specs=[pl.BlockSpec(memory_space=pltpu.SMEM), anywhere, vmem, vmem, vmem, vmem, anywhere],
        out_specs=vmem,
        scratch_shapes=[
            pltpu.VMEM((SETS, 8, LANES), jnp.int32),
            pltpu.VMEM((N * N, LANES), F32),
            pltpu.VMEM((33, 2 * N, LANES), F32),
            pltpu.VMEM((5, 8, 2, 8, LANES), F32),
            pltpu.VMEM((SETS, STRIPS, 2, 2 * N, LANES), BF16),
            pltpu.VMEM((SETS, STRIPS, 2, 2 * N, LANES), BF16),
            pltpu.VMEM((CELLS, LANES), F32),
            pltpu.VMEM((4, 8, 2, 16, LANES), F32),
            pltpu.VMEM((G, LANES), F32),
            pltpu.VMEM((SETS, G, LANES), BF16),
            pltpu.VMEM((SETS, XS, ROWS, LANES), BF16),
            pltpu.VMEM((ROWS, 4 * EIG), BF16),
            pltpu.VMEM((BANDS, PAIRS, 4 * EIG), F32),
            pltpu.VMEM((8, BANDS, 8, 4 * EIG), F32),
            pltpu.VMEM((BANDS, 8, 4 * EIG), F32),
            pltpu.VMEM((16, 8, 2 * EIG), F32),
            dma((2,)),
            dma((SETS, STRIPS)),
            dma((SETS, STRIPS)),
            dma((4,)),
            dma((2,)),
            dma((2,)),
            dma((SETS, 3)),
            dma((SETS, 3)),
            dma((BANDS, 8)),
            dma((8, BANDS)),
            dma((BANDS, 2)),
            dma((16,)),
        ],
        compiler_params=pltpu.CompilerParams(
            collective_id=0, has_side_effects=True, vmem_limit_bytes=VMEM_LIMIT
        ),
        name="projections",
    )(g_cell, pairs, occ, emp, jnp.asarray(t1), jnp.asarray(t2), eigvecs)


def shards(occupied, empty, pair_occ, pair_emp, g_cell, eigvecs):
    occ = jnp.transpose(occupied, (1, 2, 3, 0)).reshape(2, N * N, LANES)
    emp = jnp.transpose(empty, (1, 2, 3, 0)).reshape(2, N * N, LANES)
    rows = [jnp.concatenate([pair_occ, pair_occ]), jnp.concatenate([pair_emp, pair_emp])]
    pairs = jnp.stack(rows + [jnp.zeros_like(rows[0])] * 6)
    return run(g_cell, pairs, occ, emp, eigvecs)


def solution(mesh):
    in_specs = (
        P(None, "grid", None, None),
        P(None, "grid", None, None),
        P("band"),
        P("band"),
        P("grid"),
        P(None, "grid", "band"),
    )
    out_specs = P(None, "grid", "band")
    return jax.shard_map(shards, mesh=mesh, in_specs=in_specs, out_specs=out_specs, check_vma=False)
```

time: 607 us -> 132 us (0.22)
  the two profiles are of different devices: /device:TPU:2 before, /device:TPU:241 now
where the time goes in v2:
time: 132 us; the launch traced here: 130 us
  Pallas kernels  127 us (96%)
  local copies, waits for them, and re-layouts  1.53 us (1%)
  other arithmetic  1.47 us (1%)
    pallas_call x1, Pallas kernels, run(): pl.pallas_call(kernel, out_shape=jax.ShapeDtypeStruct((2, 16, EIG), F32),...  127 us

profile of v2, /device:TPU:241, one launch (start us, length us, event | category | flops | bytes accessed | tf_op | source)
XLA Modules:
  0.0 129.8 jit_solution(10167239750982040276)
XLA Ops:
  0.0 0.1 pad.3.clone
  0.1 0.1 pad.2.clone
  0.2 0.8 add_bitcast_fusion
  1.0 0.7 add_add_fusion.pairs_ref
  1.6 126.8 %projections.1 = f32[2,16,256]{2,1,0:T(8,128)} custom-call(s32[3840]{0:T(1024)} %cell_ref.1, s32[8,128]{1,0:T(8,128)} %add_add_fusion.pairs_ref, bf16[2,4096,128]{2,1,0:T(8,128)(2,1)} %bitcast.10, bf16[2,4096,128]{2,1,0:T(8,128)(2,1)} %bitcast.11, bf16[256,256]{1,0:T(8,128)(2,1)} %constant.2.clone.t1_ref, bf16[256,128]{1,0:T(8,128)(2,1)} %constant.8.clone.t2_ref, ...), custom_call_target="tpu_custom_call" | custom-call | tf_op jit(solution)/shard_map/projections/pallas_call | solution.py:484
  128.5 1.4 %copy.10 = f32[2,16,256]{2,1,0:T(8,128)} copy(f32[2,16,256]{2,1,0:T(8,128)} %projections.1) | data formatting | bytes 65536
  (2 shorter events, 0.0 us)

commit v3 on v2

--- a/solution.py
+++ b/solution.py
@@ -184,24 +184,21 @@
                     cells[pl.ds((kx + 32) * LANES + cell, 8), :] = even - odd
 
 
-def pick(cell_ref, cells, rows, out):
-    block = 16
-
-    @pl.loop(0, G // block)
+def pick(cell_ref, cells, rows, out, part):
+    block = 128
+
+    @pl.loop(0, ROWS // block)
     def _(step):
-        at = pl.multiple_of(step * block, block)
+        at = pl.multiple_of(part * ROWS + step * block, block)
         for i in range(block):
-            rows[pl.ds(at + i, 1), :] = cells[pl.ds(cell_ref[at + i], 1), :]
-
-    @pl.loop(0, G // 128)
-    def _(step):
-        at = pl.ds(pl.multiple_of(step * 128, 128), 128)
-        out[at, :] = rows[at, :].astype(BF16)
+            rows[i : i + 1, :] = cells[pl.ds(cell_ref[at + i], 1), :]
+        out[pl.ds(at, block), :] = rows[...].astype(BF16)
 
 
 def kernel(
-    cell_ref, pairs_ref, occ_ref, emp_ref, t1_ref, t2_ref, eig_ref, out,
-    lists, dens, spec, work_y, send, recv, cells, work_x, rows, own, held, eigs, sums, parts, done, final,
+    cell_ref, pocc_ref, pemp_ref, occ_any, emp_any, t1_ref, t2_ref, eig_ref, out,
+    occ_ref, emp_ref, lists, dens, spec, work_y, send, recv, cells, work_x, rows, own, held, eigs, sums, parts,
+    done, final0, final1,
     list_sems, a_send, a_recv, local_sems, e_send, e_recv, x_send, x_recv, r_send, r_recv, f_send, f_recv,
 ):
     band = lax.axis_index("band")
@@ -222,7 +219,7 @@
         return (2 * ((x + step) % XS) + zh, me)
 
     partner_z = (band + 1 - 2 * zh, me)
-    partner_x = (band + 2 - 4 * half, me)
+    beside = [(2 * ((x + 1 - 2 * half) % XS) + zh, me), (2 * ((x + 3 + 2 * half) % XS) + zh, me)]
 
     barrier = pltpu.get_barrier_semaphore()
 
@@ -234,6 +231,21 @@
             src_ref=src, dst_ref=dst, send_sem=send_sem, recv_sem=recv_sem, device_id=device, device_id_type=MESH
         )
 
+    slabs = [
+        pltpu.make_async_copy(occ_any, occ_ref, local_sems.at[0]),
+        pltpu.make_async_copy(emp_any, emp_ref, local_sems.at[1]),
+    ]
+    own_at = pl.ds(pl.multiple_of(half * ROWS, ROWS), ROWS)
+    other_at = pl.ds(pl.multiple_of((1 - half) * ROWS, ROWS), ROWS)
+    eig_own = [
+        pltpu.make_async_copy(
+            eig_ref.at[i, own_at], eigs.at[:, pl.ds(i * EIG, EIG)], local_sems.at[2 + i]
+        )
+        for i in range(2)
+    ]
+    for copy in slabs + eig_own:
+        copy.start()
+
     @pl.loop(1, STRIPS)
     def _(k):
         greet(peer((me + k) % STRIPS))
@@ -242,44 +254,42 @@
     for step in (1, 2, 3):
         greet(along_x(step))
 
-    @pl.loop(0, 16)
+    @pl.loop(0, 8)
     def _(k):
-        source = (k // 4) * 8 + 2 * (low % 4) + k % 2
-        to = 2 * (2 * (x // 2) + (k // 2) % 2) + zh
-
-        @pl.when(jnp.logical_or(source != me, to != band))
+        source = (k // 2) * 8 + 2 * (low % 4) + k % 2
+        greet((beside[0][0], source))
+        greet((beside[1][0], source))
+
+        @pl.when(source != me)
         def _():
-            greet((to, source))
+            greet((band, source))
 
     mine = jnp.where(jnp.logical_or(low == 0, low == 7), 1, 0)
-    list_own = pltpu.make_async_copy(pairs_ref, lists.at[zh], local_sems.at[0])
-    list_own.start()
-    eig_own = [
-        pltpu.make_async_copy(
-            eig_ref.at[i, pl.ds(pl.multiple_of(half * ROWS, ROWS), ROWS)],
-            eigs.at[:, pl.ds(pl.multiple_of(half * 2 * EIG + i * EIG, EIG), EIG)],
-            local_sems.at[1 + i],
-        )
-        for i in range(2)
-    ]
-    for copy in eig_own:
-        copy.start()
-    list_own.wait()
-    pl.semaphore_wait(barrier, 31 + 1 + 3 + 16 - mine)
+
+    def prepare(which):
+        density(occ_ref, emp_ref, lists[which], dens)
+        transform_y(dens, spec.at[which], work_y)
+
+    lists[zh, 0:1, :] = jnp.concatenate([pocc_ref[...], pocc_ref[...]], axis=1)
+    lists[zh, 1:2, :] = jnp.concatenate([pemp_ref[...], pemp_ref[...]], axis=1)
+    lists[zh, 2:8, :] = jnp.zeros((6, LANES), jnp.int32)
+    for copy in slabs:
+        copy.wait()
+    prepare(zh)
+    pl.semaphore_wait(barrier, 31 + 1 + 3 + 24 - mine)
 
     list_copy = remote(lists.at[zh], lists.at[zh], list_sems.at[0], list_sems.at[1], partner_z)
     list_copy.start()
     eig_copy = [
         remote(
-            eig_ref.at[i, pl.ds(pl.multiple_of((1 - half) * ROWS, ROWS), ROWS)],
-            eigs.at[:, pl.ds(pl.multiple_of(half * 2 * EIG + i * EIG, EIG), EIG)],
-            e_send.at[i], e_recv.at[i], partner_x,
+            eig_ref.at[i, other_at, pl.ds(k * 128, 128)], eigs.at[:, pl.ds(512 + k * 256 + i * 128, 128)],
+            e_send.at[k, i], e_recv.at[k, i], beside[k],
         )
+        for k in range(2)
         for i in range(2)
     ]
     for copy in eig_copy:
         copy.start()
-    list_copy.wait()
 
     def a_copy(which, strip):
         return remote(
@@ -287,9 +297,6 @@
         )
 
     def planes(which):
-        density(occ_ref, emp_ref, lists[which], dens)
-        transform_y(dens, spec, work_y)
-
         def start(strip):
             @pl.when(strip != me)
             def _():
@@ -300,8 +307,8 @@
         @pl.loop(0, 16)
         def _(step):
             j = (me + step) % 16
-            h0, l0 = split(spec[2 * j])
-            h1, l1 = split(spec[2 * j + 1])
+            h0, l0 = split(spec[which, 2 * j])
+            h1, l1 = split(spec[which, 2 * j + 1])
             high = jnp.concatenate([h0, h1], axis=1)
             low_part = jnp.concatenate([l0, l1], axis=1)
             both = dot(t1_ref[...], jnp.concatenate([high, low_part], axis=0)) + dot(t2_ref[...], high)
@@ -316,7 +323,7 @@
 
             send[which, 31 - j, 1] = both[LANES:, LANES:]
 
-        h0, l0 = split(spec[32])
+        h0, l0 = split(spec[which, 32])
         one = dot(t1_ref[:LANES, :], jnp.concatenate([h0, l0], axis=0)) + dot(t2_ref[:LANES, :], h0)
         send[which, 16, 0] = one.astype(BF16)
 
@@ -324,7 +331,7 @@
         def _(step):
             start(16 + (me + step) % 16)
 
-        copy = pltpu.make_async_copy(send.at[which, me], recv.at[which, me], local_sems.at[3])
+        copy = pltpu.make_async_copy(send.at[which, me], recv.at[which, me], local_sems.at[4])
         copy.start()
         copy.wait()
 
@@ -345,9 +352,10 @@
             ).wait_recv()
 
         transform_x(recv.at[which], cells, work_x)
-        pick(cell_ref, cells, rows, own.at[which])
-        for step in (1, 3, 2):
-            x_copy(which, step).start()
+        pick(cell_ref, cells, rows, own.at[which], 1 - half)
+        x_copy(which, 1).start()
+        x_copy(which, 3).start()
+        pick(cell_ref, cells, rows, own.at[which], half)
 
     def r_copy(block, to):
         return remote(
@@ -356,43 +364,46 @@
         )
 
     def multiply(src, block):
-        @pl.loop(0, 2)
-        def _(q):
-            at = pl.multiple_of(q * 2 * EIG, 2 * EIG)
+        for q in range(2):
+            base = q * 2 * EIG
             part = lax.dot_general(
-                src[...], eigs[:, pl.ds(at, 2 * EIG)], (((0,), (0,)), ((), ())), preferred_element_type=F32
+                src[...], eigs[:, base : base + 2 * EIG], (((0,), (0,)), ((), ())), preferred_element_type=F32
             )
-            sums[block, :, pl.ds(at, EIG)] = part[:PAIRS, :EIG] + part[PAIRS:, EIG:]
-            sums[block, :, pl.ds(at + EIG, EIG)] = part[:PAIRS, EIG:] - part[PAIRS:, :EIG]
+            wide = EIG if q == 0 else EIG // 2
+            for at in range(0, 2 * EIG, 2 * wide):
+                first, second = slice(at, at + wide), slice(at + wide, at + 2 * wide)
+                sums[block, :, base + at : base + at + wide] = part[:PAIRS, first] + part[PAIRS:, second]
+                sums[block, :, base + at + wide : base + at + 2 * wide] = part[:PAIRS, second] - part[PAIRS:, first]
 
         @pl.loop(1, 8)
         def _(k):
             r_copy(block, (low + k) % 8).start()
 
     def multiply_own(which):
-        at = pl.ds(pl.multiple_of(half * ROWS, ROWS), ROWS)
-        multiply(own.at[which, at], 2 * x + which)
+        multiply(own.at[which, own_at], 2 * x + which)
 
     def multiply_from(which, step):
         x_copy(which, step).wait_recv()
         source = (x - step + XS) % XS
         multiply(held.at[which, source], 2 * source + which)
 
+    def owner(block):
+        return (block // 2) * 8 + 4 * (block % 2) + low // 2
+
+    slot = zl * 2 + low % 2
+
     def f_copy(block, q):
-        owner = (block // 2) * 8 + 4 * (block % 2) + low // 2
-        slot = (zl * 2 + half) * 2 + low % 2
-        return remote(
-            done.at[block, :, pl.ds(q * 2 * EIG, 2 * EIG)], final.at[slot],
-            f_send.at[block, q], f_recv.at[slot], (2 * (2 * (x // 2) + q) + zh, owner),
-        )
-
-    def here(block, q):
-        owner = (block // 2) * 8 + 4 * (block % 2) + low // 2
-        return jnp.logical_and(owner == me, half == q)
-
-    def reduce(which):
-        @pl.loop(0, XS)
-        def _(step):
+        if q == 0:
+            src, dst, to = done.at[block, :, pl.ds(0, 512)], final0.at[slot], band
+        else:
+            src, dst = done.at[block, :, pl.ds(256 + 256 * q, 256)], final1.at[q - 1, slot]
+            to = beside[q - 1][0]
+        return remote(src, dst, f_send.at[block, q], f_recv.at[q, slot], (to, owner(block)))
+
+    def reduce(which, first, last):
+        @pl.loop(first, last)
+        def _(k):
+            step = k + k // 2 - 2 * (k // 3)
             block = 2 * ((x + XS - step) % XS) + which
             mine_at = pl.ds(pl.multiple_of(low * 8, 8), 8)
 
@@ -405,21 +416,33 @@
                 return total + parts[source, block]
 
             done[block] = lax.fori_loop(1, 8, add, sums[block, mine_at, :])
-            for q in range(2):
-                local = here(block, q)
-
-                @pl.when(jnp.logical_not(local))
-                def _():
-                    f_copy(block, q).start()
-
-                @pl.when(local)
-                def _():
-                    slot = (zl * 2 + half) * 2 + low % 2
-                    final[slot] = done[block, :, q * 2 * EIG : (q + 1) * 2 * EIG]
+            f_copy(block, 1).start()
+            f_copy(block, 2).start()
+            local = owner(block) == me
+
+            @pl.when(jnp.logical_not(local))
+            def _():
+                f_copy(block, 0).start()
+
+            @pl.when(local)
+            def _():
+                final0[slot] = done[block, :, :512]
+
+    @pl.when(zh == 1)
+    def _():
+        list_copy.wait()
+        prepare(0)
 
     planes(0)
+
+    @pl.when(zh == 0)
+    def _():
+        list_copy.wait()
+        prepare(1)
+
     planes(1)
     columns(0)
+    x_copy(0, 2).start()
     for copy in eig_own:
         copy.wait()
     for copy in eig_copy:
@@ -429,29 +452,41 @@
     multiply_own(1)
     for step in (1, 3, 2):
         multiply_from(0, step)
+    x_copy(1, 1).wait_send()
+    x_copy(1, 3).wait_send()
+    x_copy(1, 2).start()
     multiply_from(1, 1)
     multiply_from(1, 3)
-    reduce(0)
+    reduce(0, 0, 4)
+    reduce(1, 0, 3)
     multiply_from(1, 2)
-    reduce(1)
+    reduce(1, 3, 4)
 
     for row in range(2):
         total = jnp.zeros((8, 2 * EIG), F32)
-        for k in range(8):
-            slot = 2 * k + row
+        ends = [jnp.zeros((8, EIG), F32)] * 2
+        for k in range(4):
+            at = 2 * k + row
             local = jnp.logical_and(
-                jnp.logical_and(zl * 2 + half == k, low % 2 == row), jnp.logical_or(low == 0, low == 7)
+                jnp.logical_and(zl == k, low % 2 == row), jnp.logical_or(low == 0, low == 7)
             )
 
             @pl.when(jnp.logical_not(local))
             def _():
+                remote(final0.at[at], final0.at[at], f_send.at[0, 0], f_recv.at[0, at], partner_z).wait_recv()
+
+            total = total + final0[at]
+            for q in range(2):
                 remote(
-                    final.at[slot], final.at[slot], f_send.at[0, 0], f_recv.at[slot], partner_x
+                    final1.at[q, at], final1.at[q, at], f_send.at[0, 0], f_recv.at[1 + q, at], partner_z
                 ).wait_recv()
-
-            total = total + final[slot]
-        out[0, 8 * row : 8 * row + 8, :] = total[:, :EIG]
-        out[1, 8 * row : 8 * row + 8, :] = total[:, EIG:]
+                ends[q] = ends[q] + final1[q, at]
+        for i in range(2):
+            for q in range(2):
+                base = i * EIG + q * 128
+                out[i, 8 * row : 8 * row + 8, q * 128 : q * 128 + 128] = (
+                    total[:, base : base + 128] + ends[q][:, i * 128 : i * 128 + 128]
+                )
 
     for copy in eig_copy:
         copy.wait_send()
@@ -460,9 +495,9 @@
     def _(k):
         a_copy(1, (me + k) % STRIPS).wait_send()
 
-    for which in range(SETS):
-        for step in (1, 2, 3):
-            x_copy(which, step).wait_send()
+    for step in (1, 2, 3):
+        x_copy(0, step).wait_send()
+    x_copy(1, 2).wait_send()
 
     @pl.loop(0, BANDS)
     def _(block):
@@ -470,13 +505,15 @@
         def _(k):
             r_copy(block, (low + k) % 8).wait_send()
 
-        for q in range(2):
-            @pl.when(jnp.logical_not(here(block, q)))
-            def _():
-                f_copy(block, q).wait_send()
-
-
-def run(g_cell, pairs, occ, emp, eigvecs):
+        f_copy(block, 1).wait_send()
+        f_copy(block, 2).wait_send()
+
+        @pl.when(owner(block) != me)
+        def _():
+            f_copy(block, 0).wait_send()
+
+
+def run(g_cell, pocc, pemp, occ, emp, eigvecs):
     t1, t2 = z_tables()
     vmem = pl.BlockSpec(memory_space=pltpu.VMEM)
     anywhere = pl.BlockSpec(memory_space=pl.ANY)
@@ -484,51 +521,52 @@
     return pl.pallas_call(
         kernel,
         out_shape=jax.ShapeDtypeStruct((2, 16, EIG), F32),
-        in_specs=[pl.BlockSpec(memory_space=pltpu.SMEM), anywhere, vmem, vmem, vmem, vmem, anywhere],
+        in_specs=[pl.BlockSpec(memory_space=pltpu.SMEM), vmem, vmem, anywhere, anywhere, vmem, vmem, anywhere],
         out_specs=vmem,
         scratch_shapes=[
+            pltpu.VMEM((2, N * N, LANES), BF16),
+            pltpu.VMEM((2, N * N, LANES), BF16),
             pltpu.VMEM((SETS, 8, LANES), jnp.int32),
             pltpu.VMEM((N * N, LANES), F32),
-            pltpu.VMEM((33, 2 * N, LANES), F32),
+            pltpu.VMEM((SETS, 33, 2 * N, LANES), F32),
             pltpu.VMEM((5, 8, 2, 8, LANES), F32),
             pltpu.VMEM((SETS, STRIPS, 2, 2 * N, LANES), BF16),
             pltpu.VMEM((SETS, STRIPS, 2, 2 * N, LANES), BF16),
             pltpu.VMEM((CELLS, LANES), F32),
             pltpu.VMEM((4, 8, 2, 16, LANES), F32),
-            pltpu.VMEM((G, LANES), F32),
+            pltpu.VMEM((128, LANES), F32),
             pltpu.VMEM((SETS, G, LANES), BF16),
             pltpu.VMEM((SETS, XS, ROWS, LANES), BF16),
             pltpu.VMEM((ROWS, 4 * EIG), BF16),
             pltpu.VMEM((BANDS, PAIRS, 4 * EIG), F32),
             pltpu.VMEM((8, BANDS, 8, 4 * EIG), F32),
             pltpu.VMEM((BANDS, 8, 4 * EIG), F32),
-            pltpu.VMEM((16, 8, 2 * EIG), F32),
+            pltpu.VMEM((8, 8, 2 * EIG), F32),
+            pltpu.VMEM((2, 8, 8, EIG), F32),
             dma((2,)),
             dma((SETS, STRIPS)),
             dma((SETS, STRIPS)),
-            dma((4,)),
-            dma((2,)),
-            dma((2,)),
+            dma((5,)),
+            dma((2, 2)),
+            dma((2, 2)),
             dma((SETS, 3)),
             dma((SETS, 3)),
             dma((BANDS, 8)),
             dma((8, BANDS)),
-            dma((BANDS, 2)),
-            dma((16,)),
+            dma((BANDS, 3)),
+            dma((3, 8)),
         ],
         compiler_params=pltpu.CompilerParams(
             collective_id=0, has_side_effects=True, vmem_limit_bytes=VMEM_LIMIT
         ),
         name="projections",
-    )(g_cell, pairs, occ, emp, jnp.asarray(t1), jnp.asarray(t2), eigvecs)
+    )(g_cell, pocc, pemp, occ, emp, jnp.asarray(t1), jnp.asarray(t2), eigvecs)
 
 
 def shards(occupied, empty, pair_occ, pair_emp, g_cell, eigvecs):
     occ = jnp.transpose(occupied, (1, 2, 3, 0)).reshape(2, N * N, LANES)
     emp = jnp.transpose(empty, (1, 2, 3, 0)).reshape(2, N * N, LANES)
-    rows = [jnp.concatenate([pair_occ, pair_occ]), jnp.concatenate([pair_emp, pair_emp])]
-    pairs = jnp.stack(rows + [jnp.zeros_like(rows[0])] * 6)
-    return run(g_cell, pairs, occ, emp, eigvecs)
+    return run(g_cell, pair_occ.reshape(1, PAIRS), pair_emp.reshape(1, PAIRS), occ, emp, eigvecs)
 
 
 def solution(mesh):

time: 132 us -> 132 us (level); the launches traced: 130 us -> 132 us
  Pallas kernels: 127 us -> 131 us
  other arithmetic: 1.47 us -> 0 us
    pallas_call x1, Pallas kernels: 127 us -> 131 us  [run(): pl.pallas_call(kernel, out_shape=jax.ShapeDtypeStruct((2, 16, EIG), F32),...]
    another operation x2 -> x0, other arithmetic: 1.47 us -> none  [shards(): pairs = jnp.stack(rows + [jnp.zeros_like(rows[0])] * 6)]
where the time goes in v3:
time: 132 us
  Pallas kernels  131 us (99%)
  local copies, waits for them, and re-layouts  1.38 us (1%)
    pallas_call x1, Pallas kernels, run(): pl.pallas_call(kernel, out_shape=jax.ShapeDtypeStruct((2, 16, EIG), F32),...  131 us

profile of v3, /device:TPU:241, one launch (start us, length us, event | category | flops | bytes accessed | tf_op | source)
XLA Modules:
  0.0 132.2 jit_solution(10324529120438188126)
XLA Ops:
  0.0 130.8 %projections.1 = f32[2,16,256]{2,1,0:T(8,128)} custom-call(s32[3840]{0:T(1024)} %cell_ref.1, s32[1,64]{1,0:T(1,128)} %bitcast.10, s32[1,64]{1,0:T(1,128)} %bitcast.11, bf16[2,4096,128]{2,1,0:T(8,128)(2,1)} %bitcast.8, bf16[2,4096,128]{2,1,0:T(8,128)(2,1)} %bitcast.9, bf16[256,256]{1,0:T(8,128)(2,1)} %constant.4.clone.t1_ref, ...), custom_call_target="tpu_custom_call" | custom-call | tf_op jit(solution)/shard_map/projections/pallas_call | solution.py:521
  130.8 1.4 %copy.10 = f32[2,16,256]{2,1,0:T(8,128)} copy(f32[2,16,256]{2,1,0:T(8,128)} %projections.1) | data formatting | bytes 65536

commit v4 on v3

--- a/solution.py
+++ b/solution.py
@@ -291,18 +291,20 @@
     for copy in eig_copy:
         copy.start()
 
-    def a_copy(which, strip):
+    def a_copy(phase, strip):
+        device = peer(strip)
+        pairs = (device[0] + phase) % 2
         return remote(
-            send.at[which, strip], recv.at[which, me], a_send.at[which, strip], a_recv.at[which, me], peer(strip)
+            send.at[pairs, strip], recv.at[phase, me], a_send.at[STRIPS if phase else strip], a_recv.at[phase], device
         )
 
-    def planes(which):
+    def planes(which, near):
         def start(strip):
-            @pl.when(strip != me)
+            same = peer(strip)[0] % 2 == zh
+
+            @pl.when(jnp.logical_and(same, strip != me) if near else jnp.logical_not(same))
             def _():
-                if which:
-                    a_copy(0, strip).wait_send()
-                a_copy(which, strip).start()
+                a_copy(0, strip).start()
 
         @pl.loop(0, 16)
         def _(step):
@@ -316,24 +318,24 @@
             send[which, j, 0] = both[:LANES, :LANES]
             send[which, j, 1] = both[:LANES, LANES:]
             start(j)
+            send[which, 31 - j, 1] = both[LANES:, LANES:]
 
             @pl.when(j > 0)
             def _():
                 send[which, 32 - j, 0] = both[LANES:, :LANES]
 
-            send[which, 31 - j, 1] = both[LANES:, LANES:]
+                @pl.when(step > 0)
+                def _():
+                    start(32 - j)
 
         h0, l0 = split(spec[which, 32])
         one = dot(t1_ref[:LANES, :], jnp.concatenate([h0, l0], axis=0)) + dot(t2_ref[:LANES, :], h0)
         send[which, 16, 0] = one.astype(BF16)
-
-        @pl.loop(0, 16)
-        def _(step):
-            start(16 + (me + step) % 16)
-
-        copy = pltpu.make_async_copy(send.at[which, me], recv.at[which, me], local_sems.at[4])
-        copy.start()
-        copy.wait()
+        start(16)
+
+        @pl.when(me % 16 > 0)
+        def _():
+            start(32 - me % 16)
 
     def x_copy(which, step):
         part = half if step == 2 else 1 - half
@@ -343,14 +345,8 @@
         )
 
     def columns(which):
-        @pl.loop(1, STRIPS)
-        def _(k):
-            source = (me + k) % STRIPS
-            remote(
-                send.at[which, source], recv.at[which, source], a_send.at[which, source],
-                a_recv.at[which, source], peer(source),
-            ).wait_recv()
-
+        got = recv.at[which, pl.ds(0, STRIPS - 1)]
+        remote(got, got, a_send.at[0], a_recv.at[which], partner_z).wait_recv()
         transform_x(recv.at[which], cells, work_x)
         pick(cell_ref, cells, rows, own.at[which], 1 - half)
         x_copy(which, 1).start()
@@ -359,8 +355,8 @@
 
     def r_copy(block, to):
         return remote(
-            sums.at[block, pl.ds(pl.multiple_of(to * 8, 8), 8)], parts.at[low, block],
-            r_send.at[block, to], r_recv.at[low, block], (band, zl * 8 + to),
+            sums.at[block, pl.ds(pl.multiple_of(to * 8, 8), 8)], parts.at[block, low],
+            r_send.at[0], r_recv.at[block], (band, zl * 8 + to),
         )
 
     def multiply(src, block):
@@ -380,12 +376,12 @@
             r_copy(block, (low + k) % 8).start()
 
     def multiply_own(which):
-        multiply(own.at[which, own_at], 2 * x + which)
+        multiply(own.at[which, own_at], 2 * x + (zh + which) % 2)
 
     def multiply_from(which, step):
         x_copy(which, step).wait_recv()
         source = (x - step + XS) % XS
-        multiply(held.at[which, source], 2 * source + which)
+        multiply(held.at[which, source], 2 * source + (zh + which) % 2)
 
     def owner(block):
         return (block // 2) * 8 + 4 * (block % 2) + low // 2
@@ -398,24 +394,21 @@
         else:
             src, dst = done.at[block, :, pl.ds(256 + 256 * q, 256)], final1.at[q - 1, slot]
             to = beside[q - 1][0]
-        return remote(src, dst, f_send.at[block, q], f_recv.at[q, slot], (to, owner(block)))
+        return remote(src, dst, f_send.at[min(q, 1)], f_recv.at[min(q, 1)], (to, owner(block)))
 
     def reduce(which, first, last):
         @pl.loop(first, last)
         def _(k):
             step = k + k // 2 - 2 * (k // 3)
-            block = 2 * ((x + XS - step) % XS) + which
+            block = 2 * ((x + XS - step) % XS) + (zh + which) % 2
             mine_at = pl.ds(pl.multiple_of(low * 8, 8), 8)
 
-            def add(k, total):
-                source = (low + k) % 8
-                remote(
-                    sums.at[block, mine_at], parts.at[source, block], r_send.at[block, source],
-                    r_recv.at[source, block], (band, zl * 8 + source),
-                ).wait_recv()
-                return total + parts[source, block]
-
-            done[block] = lax.fori_loop(1, 8, add, sums[block, mine_at, :])
+            got = parts.at[block, pl.ds(0, 7)]
+            remote(got, got, r_send.at[0], r_recv.at[block], partner_z).wait_recv()
+            total = sums[block, mine_at, :]
+            for i in range(1, 8):
+                total = total + parts[block, (low + i) % 8]
+            done[block] = total
             f_copy(block, 1).start()
             f_copy(block, 2).start()
             local = owner(block) == me
@@ -428,19 +421,24 @@
             def _():
                 final0[slot] = done[block, :, :512]
 
-    @pl.when(zh == 1)
-    def _():
-        list_copy.wait()
-        prepare(0)
-
-    planes(0)
-
-    @pl.when(zh == 0)
-    def _():
-        list_copy.wait()
-        prepare(1)
-
-    planes(1)
+    planes(zh, True)
+    list_copy.wait()
+    prepare(1 - zh)
+    planes(1 - zh, False)
+    stay = [
+        pltpu.make_async_copy(send.at[(zh + phase) % 2, me], recv.at[phase, me], local_sems.at[4 + phase])
+        for phase in range(2)
+    ]
+    for copy in stay:
+        copy.start()
+
+    @pl.loop(1, STRIPS)
+    def _(k):
+        strip = (me + k // 2 + 16 * (k % 2)) % STRIPS
+        a_copy(1, strip).start()
+
+    for copy in stay:
+        copy.wait()
     columns(0)
     x_copy(0, 2).start()
     for copy in eig_own:
@@ -449,38 +447,35 @@
         copy.wait_recv()
     multiply_own(0)
     columns(1)
+    x_copy(1, 2).start()
     multiply_own(1)
     for step in (1, 3, 2):
         multiply_from(0, step)
-    x_copy(1, 1).wait_send()
-    x_copy(1, 3).wait_send()
-    x_copy(1, 2).start()
+    reduce(0, 0, 4)
     multiply_from(1, 1)
     multiply_from(1, 3)
-    reduce(0, 0, 4)
-    reduce(1, 0, 3)
     multiply_from(1, 2)
-    reduce(1, 3, 4)
-
+    reduce(1, 0, 4)
+
+    def finish(way):
+        @pl.when(mine == 1)
+        def _():
+            way(remote(final0.at[pl.ds(0, 7)], final0.at[pl.ds(0, 7)], f_send.at[0], f_recv.at[0], partner_z))
+
+        @pl.when(mine == 0)
+        def _():
+            way(remote(final0, final0, f_send.at[0], f_recv.at[0], partner_z))
+
+        way(remote(final1, final1, f_send.at[1], f_recv.at[1], partner_z))
+
+    finish(lambda copy: copy.wait_recv())
     for row in range(2):
         total = jnp.zeros((8, 2 * EIG), F32)
         ends = [jnp.zeros((8, EIG), F32)] * 2
         for k in range(4):
-            at = 2 * k + row
-            local = jnp.logical_and(
-                jnp.logical_and(zl == k, low % 2 == row), jnp.logical_or(low == 0, low == 7)
-            )
-
-            @pl.when(jnp.logical_not(local))
-            def _():
-                remote(final0.at[at], final0.at[at], f_send.at[0, 0], f_recv.at[0, at], partner_z).wait_recv()
-
-            total = total + final0[at]
+            total = total + final0[2 * k + row]
             for q in range(2):
-                remote(
-                    final1.at[q, at], final1.at[q, at], f_send.at[0, 0], f_recv.at[1 + q, at], partner_z
-                ).wait_recv()
-                ends[q] = ends[q] + final1[q, at]
+                ends[q] = ends[q] + final1[q, 2 * k + row]
         for i in range(2):
             for q in range(2):
                 base = i * EIG + q * 128
@@ -493,24 +488,17 @@
 
     @pl.loop(1, STRIPS)
     def _(k):
-        a_copy(1, (me + k) % STRIPS).wait_send()
-
+        a_copy(0, (me + k) % STRIPS).wait_send()
+
+    gone = recv.at[0, pl.ds(0, STRIPS - 1)]
+    remote(gone, gone, a_send.at[STRIPS], a_recv.at[0], partner_z).wait_send()
     for step in (1, 2, 3):
         x_copy(0, step).wait_send()
-    x_copy(1, 2).wait_send()
-
-    @pl.loop(0, BANDS)
-    def _(block):
-        @pl.loop(1, 8)
-        def _(k):
-            r_copy(block, (low + k) % 8).wait_send()
-
-        f_copy(block, 1).wait_send()
-        f_copy(block, 2).wait_send()
-
-        @pl.when(owner(block) != me)
-        def _():
-            f_copy(block, 0).wait_send()
+    for step in (1, 2, 3):
+        x_copy(1, step).wait_send()
+    gone = parts.at[pl.ds(0, 7)]
+    remote(gone, gone, r_send.at[0], r_recv.at[0], partner_z).wait_send()
+    finish(lambda copy: copy.wait_send())
 
 
 def run(g_cell, pocc, pemp, occ, emp, eigvecs):
@@ -539,22 +527,22 @@
             pltpu.VMEM((SETS, XS, ROWS, LANES), BF16),
             pltpu.VMEM((ROWS, 4 * EIG), BF16),
             pltpu.VMEM((BANDS, PAIRS, 4 * EIG), F32),
-            pltpu.VMEM((8, BANDS, 8, 4 * EIG), F32),
+            pltpu.VMEM((BANDS, 8, 8, 4 * EIG), F32),
             pltpu.VMEM((BANDS, 8, 4 * EIG), F32),
             pltpu.VMEM((8, 8, 2 * EIG), F32),
             pltpu.VMEM((2, 8, 8, EIG), F32),
             dma((2,)),
-            dma((SETS, STRIPS)),
-            dma((SETS, STRIPS)),
-            dma((5,)),
+            dma((STRIPS + 1,)),
+            dma((SETS,)),
+            dma((6,)),
             dma((2, 2)),
             dma((2, 2)),
             dma((SETS, 3)),
             dma((SETS, 3)),
-            dma((BANDS, 8)),
-            dma((8, BANDS)),
-            dma((BANDS, 3)),
-            dma((3, 8)),
+            dma((1,)),
+            dma((BANDS,)),
+            dma((2,)),
+            dma((2,)),
         ],
         compiler_params=pltpu.CompilerParams(
             collective_id=0, has_side_effects=True, vmem_limit_bytes=VMEM_LIMIT

time: 132 us -> 120 us (0.909)
  the two profiles are of different devices: /device:TPU:241 before, /device:TPU:161 now
where the time goes in v4:
time: 120 us
  Pallas kernels  119 us (99%)
  local copies, waits for them, and re-layouts  1.38 us (1%)
    pallas_call x1, Pallas kernels, run(): pl.pallas_call(kernel, out_shape=jax.ShapeDtypeStruct((2, 16, EIG), F32),...  119 us

profile of v4, /device:TPU:161, one launch (start us, length us, event | category | flops | bytes accessed | tf_op | source)
XLA Modules:
  0.0 120.3 jit_solution(6262800371339186157)
XLA Ops:
  0.0 118.9 %projections.1 = f32[2,16,256]{2,1,0:T(8,128)} custom-call(s32[3840]{0:T(1024)} %cell_ref.1, s32[1,64]{1,0:T(1,128)} %bitcast.10, s32[1,64]{1,0:T(1,128)} %bitcast.11, bf16[2,4096,128]{2,1,0:T(8,128)(2,1)} %bitcast.8, bf16[2,4096,128]{2,1,0:T(8,128)(2,1)} %bitcast.9, bf16[256,256]{1,0:T(8,128)(2,1)} %constant.4.clone.t1_ref, ...), custom_call_target="tpu_custom_call" | custom-call | tf_op jit(solution)/shard_map/projections/pallas_call | solution.py:509
  118.9 1.4 %copy.10 = f32[2,16,256]{2,1,0:T(8,128)} copy(f32[2,16,256]{2,1,0:T(8,128)} %projections.1) | data formatting | bytes 65536
